TPU v7x, 512 devices: a whole 4x4x16 slice. The times are simulated.
512 devices in a mesh: grp: 16 (over y, x_lo, core), seq: 32 (over z, x_hi).
Axes of the slice: x: 4 (x_hi: 2, x_lo: 2; x = x_hi * 2 + x_lo), y: 4, z: 16, core: 2. Of those that a mesh axis runs over, the one named last changes fastest.
Arguments:
- queries: bfloat16 [16, 4096, 1024], P('grp', 'seq'), may hold values from -8 to 8
- keys: bfloat16 [16, 4096, 1024], P('grp', 'seq'), may hold values from -8 to 8
- values: bfloat16 [16, 4096, 1024], P('grp', 'seq'), may hold values from -6 to 6
- hist_keys: bfloat16 [1024, 1024], P('grp'), may hold values from -6 to 6
- hist_values: bfloat16 [1024, 1024], P('grp'), may hold values from -6 to 6
- lengths: int32 [16], P('grp'), may hold values from 1024 to 4096, as said below
- hist_mask: int32 [16, 8], P('grp'), may hold values 0 or 1
Outputs:
- attended: bfloat16 [16, 4096, 1024], P('grp', 'seq')
Inputs may be any that keep to these rules, and one draw needn't show every extreme that they name: `lengths`: some group has all 4096 tokens live and some group only 1024.
All inputs are finite; a program needn't handle non-finite values. No bound on the sum of `hist_mask` on one device may be relied on, other than what follows from the above.
Results may differ from a plain program's by a relative error of at most 0.0043.
Values may be sent and summed in bfloat16 or wider, within the bound.
A program may use at most 64 MiB of HBM per device.

v0:
```python
import jax
import jax.numpy as jnp
from jax import lax
from jax.sharding import PartitionSpec as P

HD = 64
HBLK = 8


def attend(query_rows, key_rows, value_rows, live):
    count = query_rows.shape[0]
    block = 512
    blocks = query_rows.reshape(count // block, block, query_rows.shape[1])

    def one_block(rows):
        scores = jnp.dot(rows, key_rows.T, preferred_element_type=jnp.float32) * HD ** (-0.5)
        scores = jnp.where(live[None, :], scores, jnp.float32(-1e30))
        top = jnp.max(scores, axis=1, keepdims=True)
        weights = jnp.where(live[None, :], jnp.exp(scores - top), jnp.float32(0.0))
        total = jnp.sum(weights, axis=1, keepdims=True)
        rounded = weights.astype(jnp.bfloat16)
        mixed = jnp.dot(rounded, value_rows, preferred_element_type=jnp.float32)
        return (mixed / total).astype(jnp.bfloat16)

    return lax.map(one_block, blocks).reshape(count, value_rows.shape[1])


def body(queries, keys, values, hist_keys, hist_values, lengths, hist_mask):
    devices = lax.axis_size("seq")
    tok = queries.shape[1]
    heads = queries.shape[2] // HD
    half = tok // 2
    local_q = (
        queries[0].reshape(2, half, heads, HD).transpose(2, 0, 1, 3).reshape(heads * 2, half, HD)
    )
    head_q = lax.all_to_all(local_q, "seq", split_axis=0, concat_axis=1, tiled=True)
    items = head_q.shape[0]
    local_k = keys[0].reshape(tok, heads, HD).transpose(1, 0, 2)
    local_v = values[0].reshape(tok, heads, HD).transpose(1, 0, 2)
    twice_k = jnp.broadcast_to(local_k[:, None], (heads, 2, tok, HD)).reshape(heads * 2, tok, HD)
    twice_v = jnp.broadcast_to(local_v[:, None], (heads, 2, tok, HD)).reshape(heads * 2, tok, HD)
    item_k, item_v = (
        lax.all_to_all(twice_k, "seq", split_axis=0, concat_axis=1, tiled=True),
        lax.all_to_all(twice_v, "seq", split_axis=0, concat_axis=1, tiled=True),
    )
    key_pos = jnp.arange(devices * tok, dtype=jnp.int32)
    first_item = lax.axis_index("seq") * items
    head_count = max(1, items // 2)
    start_col = first_item // 2 * HD
    slice_k = lax.dynamic_slice_in_dim(hist_keys, start_col, head_count * HD, 1)
    slice_v = lax.dynamic_slice_in_dim(hist_values, start_col, head_count * HD, 1)
    all_hk, all_hv = (
        lax.all_gather(slice_k, "grp", axis=0, tiled=True),
        lax.all_gather(slice_v, "grp", axis=0, tiled=True),
    )
    hist_total = all_hk.shape[0]
    heads_hk = all_hk.reshape(hist_total, head_count, HD).transpose(1, 0, 2)
    heads_hv = all_hv.reshape(hist_total, head_count, HD).transpose(1, 0, 2)
    live = jnp.concatenate([key_pos < lengths[0], jnp.repeat(hist_mask[0], hist_total // HBLK) > 0])
    full_k = jnp.concatenate([item_k, heads_hk], axis=1)
    full_v = jnp.concatenate([item_v, heads_hv], axis=1)

    def one_item(operands):
        return attend(operands[0], operands[1], operands[2], live)

    head_out = lax.map(one_item, (head_q, full_k, full_v))
    returned = lax.all_to_all(head_out, "seq", split_axis=1, concat_axis=0, tiled=True)
    attended = (
        returned.reshape(heads, 2, half, HD).transpose(1, 2, 0, 3).reshape(1, tok, heads * HD)
    )
    return attended


def solution(mesh):
    return jax.shard_map(
        body,
        mesh=mesh,
        in_specs=(
            P("grp", "seq", None),
            P("grp", "seq", None),
            P("grp", "seq", None),
            P("grp", None),
            P("grp", None),
            P("grp"),
            P("grp", None),
        ),
        out_specs=P("grp", "seq", None),
        check_vma=False,
    )
```

profile of v0, /device:TPU:6, one launch (start us, length us, event | category | flops | bytes accessed | tf_op | source)
XLA Modules:
  0.0 213.1 jit_solution(15766779628654971112)
XLA Ops:
  0.0 1.4 reshape_squeeze.9
  2.6 18.2 %all-to-all-start = ((bf16[32,2,2048]{2,1,0:T(2,128)(2,1)}), bf16[32,2,2048]{2,1,0:T(2,128)(2,1)S(1)}, u32[]{:S(2)}, u32[]{:S(2)}) async-start(bf16[32,2,2048]{2,1,0:T(2,128)(2,1)} %reshape.54), calls=%async_computation | async-start | bytes 524288 | tf_op jit(solution)/shard_map/all_to_all | solution.py:36
  22.0 20.4 %all-to-all-done = bf16[32,2,2048]{2,1,0:T(2,128)(2,1)S(1)} async-done(((bf16[32,2,2048]{2,1,0:T(2,128)(2,1)}), bf16[32,2,2048]{2,1,0:T(2,128)(2,1)S(1)}, u32[]{:S(2)}, u32[]{:S(2)}) %all-to-all-start) | async-done | bytes 262176 | tf_op jit(solution)/shard_map/all_to_all | solution.py:36
  43.3 5.1 %all-to-all-start.1 = ((bf16[32,128,64]{1,2,0:T(8,128)(2,1)}), bf16[32,128,64]{1,2,0:T(8,128)(2,1)S(1)}, u32[]{:S(2)}, u32[]{:S(2)}) async-start(bf16[32,128,64]{1,2,0:T(8,128)(2,1)} %bitcast.10), calls=%async_computation.1 | async-start | bytes 1048576 | tf_op jit(solution)/shard_map/all_to_all | solution.py:43
  49.5 31.1 %all-to-all-done.1 = bf16[32,128,64]{1,2,0:T(8,128)(2,1)S(1)} async-done(((bf16[32,128,64]{1,2,0:T(8,128)(2,1)}), bf16[32,128,64]{1,2,0:T(8,128)(2,1)S(1)}, u32[]{:S(2)}, u32[]{:S(2)}) %all-to-all-start.1) | async-done | bytes 524320 | tf_op jit(solution)/shard_map/all_to_all | solution.py:43
  81.5 5.2 %all-to-all-start.2 = ((bf16[32,128,64]{1,2,0:T(8,128)(2,1)}), bf16[32,128,64]{1,2,0:T(8,128)(2,1)S(1)}, u32[]{:S(2)}, u32[]{:S(2)}) async-start(bf16[32,128,64]{1,2,0:T(8,128)(2,1)} %bitcast.15), calls=%async_computation.2 | async-start | bytes 1048576 | tf_op jit(solution)/shard_map/all_to_all | solution.py:44
  86.8 17.9 %all_gather.6 = bf16[1024,64]{1,0:T(8,128)(2,1)S(1)} all-gather(bf16[64,64]{1,0:T(8,128)(2,1)S(1)} %constant_dynamic-slice_fusion.1), channel_id=1, replica_groups=mesh['grp'=16,'seq'=32] {'grp'}, dimensions={0}, use_global_device_ids=true | all-gather | bytes 139264 | tf_op jit(solution)/shard_map/all_gather | solution.py:53
  105.7 21.1 %all_gather.7 = bf16[1024,64]{1,0:T(8,128)(2,1)S(1)} all-gather(bf16[64,64]{1,0:T(8,128)(2,1)S(1)} %constant_dynamic-slice_fusion), channel_id=1, replica_groups=mesh['grp'=16,'seq'=32] {'grp'}, dimensions={0}, use_global_device_ids=true | all-gather | bytes 139264 | tf_op jit(solution)/shard_map/all_gather | solution.py:54
  130.8 1.4 copy.52
  132.2 28.0 %while.17 = (s32[]{:T(128)}, bf16[4,512,64]{1,2,0:T(8,128)(2,1)S(1)}, pred[5120]{0:T(1024)(128)(4,1)S(1)}, bf16[4,512,64]{2,1,0:T(8,128)(2,1)S(1)}, bf16[5120,64...) while((s32[]{:T(128)}, bf16[4,512,64]{1,2,0:T(8,128)(2,1)S(1)}, pred[5120]{0:T(1024)(128)(4,1)S(1)}, ...), condition=%wide.region_3.4_spmd, body=%wide.region_0.3_spmd.sunk | while | flops 705231872 | bytes 36922480 | solution.py:25
  132.2 1.6 fusion.36
  133.8 2.9 %fusion.37 = f32[512]{0:T(512)S(1)} fusion(f32[512,5120]{1,0:T(8,128)S(1)} %get-tuple-element.121, f32[512]{0:T(512)S(1)} %get-tuple-element.122, pred[5120]{0:T(1024)(128)(4,1)S(1)} %get-tuple-element.139), kind=kLoop, calls=%fused_computation.3.clone.1 | loop fusion | flops 13106688 | bytes 10494976 | tf_op jit(solution)/shard_map/while/body/eval_jaxpr/while/body/eval_jaxpr/reduce_sum | solution.py:20
  136.7 2.4 %fusion.38 = bf16[4,512,64]{1,2,0:T(8,128)(2,1)S(1)} fusion(bf16[4,512,64]{1,2,0:T(8,128)(2,1)S(1)} %get-tuple-element.131, s32[]{:T(128)} %get-tuple-element.130, bf16[5120,64]{1,0:T(8,128)(2,1)S(1)} %copy-done.1, f32[512,5120]{1,0:T(8,128)S(1)} %get-tuple-element.121, f32[512]{0:T(512)S(1)} %get-tuple-element.122, ...), kind=kOutput, calls=%fused_computation.10.clone.1 | convolution fusion | flops 348717056 | bytes 11871236 | tf_op jit(solution)/shard_map/while/body/eval_jaxpr/while/body/eval_jaxpr/dot_general | solution.py:22
  139.2 1.6 fusion.36
  140.8 2.9 %fusion.37 = f32[512]{0:T(512)S(1)} fusion(f32[512,5120]{1,0:T(8,128)S(1)} %get-tuple-element.121, f32[512]{0:T(512)S(1)} %get-tuple-element.122, pred[5120]{0:T(1024)(128)(4,1)S(1)} %get-tuple-element.139), kind=kLoop, calls=%fused_computation.3.clone.1 | loop fusion | flops 13106688 | bytes 10494976 | tf_op jit(solution)/shard_map/while/body/eval_jaxpr/while/body/eval_jaxpr/reduce_sum | solution.py:20
  143.7 2.4 %fusion.38 = bf16[4,512,64]{1,2,0:T(8,128)(2,1)S(1)} fusion(bf16[4,512,64]{1,2,0:T(8,128)(2,1)S(1)} %get-tuple-element.131, s32[]{:T(128)} %get-tuple-element.130, bf16[5120,64]{1,0:T(8,128)(2,1)S(1)} %copy-done.1, f32[512,5120]{1,0:T(8,128)S(1)} %get-tuple-element.121, f32[512]{0:T(512)S(1)} %get-tuple-element.122, ...), kind=kOutput, calls=%fused_computation.10.clone.1 | convolution fusion | flops 348717056 | bytes 11871236 | tf_op jit(solution)/shard_map/while/body/eval_jaxpr/while/body/eval_jaxpr/dot_general | solution.py:22
  146.2 1.6 fusion.36
  147.8 2.9 %fusion.37 = f32[512]{0:T(512)S(1)} fusion(f32[512,5120]{1,0:T(8,128)S(1)} %get-tuple-element.121, f32[512]{0:T(512)S(1)} %get-tuple-element.122, pred[5120]{0:T(1024)(128)(4,1)S(1)} %get-tuple-element.139), kind=kLoop, calls=%fused_computation.3.clone.1 | loop fusion | flops 13106688 | bytes 10494976 | tf_op jit(solution)/shard_map/while/body/eval_jaxpr/while/body/eval_jaxpr/reduce_sum | solution.py:20
  150.7 2.4 %fusion.38 = bf16[4,512,64]{1,2,0:T(8,128)(2,1)S(1)} fusion(bf16[4,512,64]{1,2,0:T(8,128)(2,1)S(1)} %get-tuple-element.131, s32[]{:T(128)} %get-tuple-element.130, bf16[5120,64]{1,0:T(8,128)(2,1)S(1)} %copy-done.1, f32[512,5120]{1,0:T(8,128)S(1)} %get-tuple-element.121, f32[512]{0:T(512)S(1)} %get-tuple-element.122, ...), kind=kOutput, calls=%fused_computation.10.clone.1 | convolution fusion | flops 348717056 | bytes 11871236 | tf_op jit(solution)/shard_map/while/body/eval_jaxpr/while/body/eval_jaxpr/dot_general | solution.py:22
  153.2 1.6 fusion.36
  154.8 2.9 %fusion.37 = f32[512]{0:T(512)S(1)} fusion(f32[512,5120]{1,0:T(8,128)S(1)} %get-tuple-element.121, f32[512]{0:T(512)S(1)} %get-tuple-element.122, pred[5120]{0:T(1024)(128)(4,1)S(1)} %get-tuple-element.139), kind=kLoop, calls=%fused_computation.3.clone.1 | loop fusion | flops 13106688 | bytes 10494976 | tf_op jit(solution)/shard_map/while/body/eval_jaxpr/while/body/eval_jaxpr/reduce_sum | solution.py:20
  157.7 2.4 %fusion.38 = bf16[4,512,64]{1,2,0:T(8,128)(2,1)S(1)} fusion(bf16[4,512,64]{1,2,0:T(8,128)(2,1)S(1)} %get-tuple-element.131, s32[]{:T(128)} %get-tuple-element.130, bf16[5120,64]{1,0:T(8,128)(2,1)S(1)} %copy-done.1, f32[512,5120]{1,0:T(8,128)S(1)} %get-tuple-element.121, f32[512]{0:T(512)S(1)} %get-tuple-element.122, ...), kind=kOutput, calls=%fused_computation.10.clone.1 | convolution fusion | flops 348717056 | bytes 11871236 | tf_op jit(solution)/shard_map/while/body/eval_jaxpr/while/body/eval_jaxpr/dot_general | solution.py:22
  161.2 11.8 %reduce = bf16[2048,64]{1,0:T(8,128)(2,1)S(1)} reduce(bf16[2048,1,64]{2,1,0:T(2,128)(2,1)S(1)} %bitcast.54, bf16[]{:T(256)} %broadcast.32), dimensions={1}, to_apply=%bitcast.38.reduce_sub_computation | reduce | bytes 524290
  173.4 36.2 %all_to_all.42 = bf16[32,2,2048]{2,1,0:T(2,128)(2,1)S(1)} all-to-all(bf16[32,2,2048]{2,1,0:T(2,128)(2,1)S(1)} %reshape.56), channel_id=1, replica_groups=mesh['grp'=16,'seq'=32] {'seq'}, dimensions={0} | all-to-all | bytes 524288 | tf_op jit(solution)/shard_map/all_to_all | solution.py:67
  (43 shorter events, 14.5 us)
Async XLA Ops:
  0.0 86.7 %copy-start = (bf16[64,1024]{1,0:T(8,128)(2,1)S(1)}, bf16[64,1024]{1,0:T(8,128)(2,1)}, u32[]{:S(2)}) copy-start(bf16[64,1024]{1,0:T(8,128)(2,1)} %param.12) | copy-start | bytes 393220
  2.6 39.8 %all-to-all-start = ((bf16[32,2,2048]{2,1,0:T(2,128)(2,1)}), bf16[32,2,2048]{2,1,0:T(2,128)(2,1)S(1)}, u32[]{:S(2)}, u32[]{:S(2)}) async-start(bf16[32,2,2048]{2,1,0:T(2,128)(2,1)} %reshape.54), calls=%async_computation | async-start | bytes 524288 | tf_op jit(solution)/shard_map/all_to_all | solution.py:36
  43.3 37.3 %all-to-all-start.1 = ((bf16[32,128,64]{1,2,0:T(8,128)(2,1)}), bf16[32,128,64]{1,2,0:T(8,128)(2,1)S(1)}, u32[]{:S(2)}, u32[]{:S(2)}) async-start(bf16[32,128,64]{1,2,0:T(8,128)(2,1)} %bitcast.10), calls=%async_computation.1 | async-start | bytes 1048576 | tf_op jit(solution)/shard_map/all_to_all | solution.py:43
  81.5 48.6 %all-to-all-start.2 = ((bf16[32,128,64]{1,2,0:T(8,128)(2,1)}), bf16[32,128,64]{1,2,0:T(8,128)(2,1)S(1)}, u32[]{:S(2)}, u32[]{:S(2)}) async-start(bf16[32,128,64]{1,2,0:T(8,128)(2,1)} %bitcast.15), calls=%async_computation.2 | async-start | bytes 1048576 | tf_op jit(solution)/shard_map/all_to_all | solution.py:44
  132.2 4.5 %copy-start.1 = (bf16[5120,64]{1,0:T(8,128)(2,1)S(1)}, bf16[5120,64]{1,0:T(8,128)(2,1)}, u32[]{:S(2)}) copy-start(bf16[5120,64]{1,0:T(8,128)(2,1)} %get-tuple-element.142) | copy-start | bytes 1966084 | tf_op jit(solution)/shard_map/while/body/eval_jaxpr/while
  139.2 4.5 %copy-start.1 = (bf16[5120,64]{1,0:T(8,128)(2,1)S(1)}, bf16[5120,64]{1,0:T(8,128)(2,1)}, u32[]{:S(2)}) copy-start(bf16[5120,64]{1,0:T(8,128)(2,1)} %get-tuple-element.142) | copy-start | bytes 1966084 | tf_op jit(solution)/shard_map/while/body/eval_jaxpr/while
  146.2 4.5 %copy-start.1 = (bf16[5120,64]{1,0:T(8,128)(2,1)S(1)}, bf16[5120,64]{1,0:T(8,128)(2,1)}, u32[]{:S(2)}) copy-start(bf16[5120,64]{1,0:T(8,128)(2,1)} %get-tuple-element.142) | copy-start | bytes 1966084 | tf_op jit(solution)/shard_map/while/body/eval_jaxpr/while
  153.2 4.5 %copy-start.1 = (bf16[5120,64]{1,0:T(8,128)(2,1)S(1)}, bf16[5120,64]{1,0:T(8,128)(2,1)}, u32[]{:S(2)}) copy-start(bf16[5120,64]{1,0:T(8,128)(2,1)} %get-tuple-element.142) | copy-start | bytes 1966084 | tf_op jit(solution)/shard_map/while/body/eval_jaxpr/while
where the time goes:
time: 214 us; the launch traced here: 213 us
  blocking collectives  75.2 us (35%)
  waiting for transfers between devices  51.5 us (24%)
  starting transfers between devices  28.5 us (13%)
  other arithmetic  24.2 us (11%)
  local copies, waits for them, and re-layouts  16.5 us (8%)
  matrix products  16.2 us (8%)
    all_to_all x1, blocking collectives, body(): lax.all_to_all(head_out, 'seq', split_axis=1, concat_axis=0, tiled=True)  36.2 us
    all_to_all x1, waiting for transfers between devices, body(): lax.all_to_all(twice_k, 'seq', split_axis=0, concat_axis=1, tiled=True)  31.1 us
    all_gather x1, blocking collectives, body(): lax.all_gather(slice_v, 'grp', axis=0, tiled=True)  21.1 us
    all_to_all x1, waiting for transfers between devices, body(): lax.all_to_all(local_q, 'seq', split_axis=0, concat_axis=1, tiled=True)  20.4 us
    all_to_all x1, starting transfers between devices, body(): lax.all_to_all(local_q, 'seq', split_axis=0, concat_axis=1, tiled=True)  18.2 us
    all_gather x1, blocking collectives, body(): lax.all_gather(slice_k, 'grp', axis=0, tiled=True)  17.9 us
    unnamed x1, other arithmetic  11.8 us
    reduce_sum x4, other arithmetic, one_block(): total = jnp.sum(weights, axis=1, keepdims=True)  11.6 us
  transfers between devices with their start and end apart: 3, of which 2 were waited for; matrix products, arithmetic and copies ran while one was open for 3% of the time, Pallas kernels for 0%

commit v1 on v0

v1 whole, which is shorter than its diff:
```python
import jax
import jax.numpy as jnp
from jax import lax
from jax.experimental import pallas as pl
from jax.experimental.pallas import tpu as pltpu
from jax.sharding import PartitionSpec as P

HD = 64
HEADS = 16
NZ = 16
TOK = 128
HALF = TOK // 2
SLOTS = 32
HROWS = 64
HIST = 1024
OWN = SLOTS * TOK
KEYS = OWN + HIST
DEAD = -1e30
MESH = pl.DeviceIdType.MESH
BF = jnp.bfloat16


def swap(x):
    return pltpu.roll(x, HD, 1)


def kernel(
    q_hbm, k_hbm, v_hbm, hk_hbm, hv_hbm, len_ref, mask_ref, o_ref,
    q_in, k_in, v_in, hk_in, hv_in,
    kv_src, kv_all, h_src, h_all, q_src, q_all, o_src, o_all,
    k2, v2, s_ref,
    in_sem, kv_ss, kv_rs, x_ss, x_rs, h_ss, h_rs, q_ss, q_rs, o_ss, o_rs,
):
    grp = lax.axis_index("grp")
    seq = lax.axis_index("seq")
    z = seq // 2
    xh = lax.rem(seq, 2)
    hcol = pl.multiple_of(z // 2 * TOK, TOK)
    odd = lax.rem(z, 2)

    loads = [
        pltpu.make_async_copy(k_hbm.at[0], k_in, in_sem.at[0]),
        pltpu.make_async_copy(v_hbm.at[0], v_in, in_sem.at[1]),
        pltpu.make_async_copy(hk_hbm.at[:, pl.ds(hcol, TOK)], hk_in, in_sem.at[2]),
        pltpu.make_async_copy(hv_hbm.at[:, pl.ds(hcol, TOK)], hv_in, in_sem.at[3]),
        pltpu.make_async_copy(q_hbm.at[0], q_in, in_sem.at[4]),
    ]
    for load in loads:
        load.start()

    def z_peer(t):
        return {"seq": t * 2 + xh}

    barrier = pltpu.get_barrier_semaphore()

    def far(i):
        return lax.rem(z + 8 + (1 - 2 * lax.rem(i, 2)) * ((i + 1) // 2), NZ)

    def greet_z(i, c):
        pl.semaphore_signal(barrier, inc=1, device_id=z_peer(far(i)), device_id_type=MESH)
        return c

    lax.fori_loop(0, NZ - 1, greet_z, 0)
    pl.semaphore_signal(barrier, inc=1, device_id={"seq": z * 2 + 1 - xh}, device_id_type=MESH)

    def greet_g(i, c):
        pl.semaphore_signal(barrier, inc=1, device_id={"grp": lax.rem(grp + i, 16)}, device_id_type=MESH)
        return c

    lax.fori_loop(1, 16, greet_g, 0)

    def lane(rows):
        return lax.broadcasted_iota(jnp.int32, (rows, TOK), 1)

    low = lane(TOK) < HD
    low_half = lane(HALF) < HD

    loads[0].wait()
    loads[1].wait()
    for c in range(HEADS // 2):
        kk = k_in[:, c * TOK : (c + 1) * TOK]
        vv = v_in[:, c * TOK : (c + 1) * TOK]
        kv_src[2 * c] = jnp.where(low, kk, swap(vv))
        kv_src[2 * c + 1] = jnp.where(low, swap(kk), vv)
    loads[2].wait()
    loads[3].wait()
    hk = hk_in[...]
    hv = hv_in[...]
    even_h = jnp.where(low_half, hk, swap(hv))
    odd_h = jnp.where(low_half, swap(hk), hv)
    pick = jnp.full((HROWS, TOK), odd, jnp.int32) == 1
    h_src[...] = jnp.where(pick, odd_h, even_h)

    pl.semaphore_wait(barrier, 31)

    def kv_copy(t, slot):
        return pltpu.make_async_remote_copy(
            src_ref=kv_src.at[t], dst_ref=kv_all.at[slot * 2 + xh],
            send_sem=kv_ss.at[t], recv_sem=kv_rs.at[slot],
            device_id=z_peer(t), device_id_type=MESH,
        )

    def x_copy(t, side):
        return pltpu.make_async_remote_copy(
            src_ref=kv_all.at[t * 2 + side], dst_ref=kv_all.at[t * 2 + side],
            send_sem=x_ss.at[t], recv_sem=x_rs.at[t],
            device_id={"seq": z * 2 + 1 - xh}, device_id_type=MESH,
        )

    def h_copy(t, slot):
        return pltpu.make_async_remote_copy(
            src_ref=h_src, dst_ref=h_all.at[slot],
            send_sem=h_ss.at[t], recv_sem=h_rs.at[slot],
            device_id={"grp": t}, device_id_type=MESH,
        )

    def q_copy(t, slot):
        return pltpu.make_async_remote_copy(
            src_ref=q_src.at[t], dst_ref=q_all.at[slot],
            send_sem=q_ss.at[t], recv_sem=q_rs.at[slot],
            device_id=z_peer(t), device_id_type=MESH,
        )

    def o_copy(t, slot):
        return pltpu.make_async_remote_copy(
            src_ref=o_src.at[t], dst_ref=o_all.at[slot],
            send_sem=o_ss.at[t], recv_sem=o_rs.at[slot],
            device_id=z_peer(t), device_id_type=MESH,
        )

    def loop(lo, hi, f):
        def step(i, c):
            f(i)
            return c

        lax.fori_loop(lo, hi, step, 0)

    loop(0, NZ - 1, lambda i: kv_copy(far(i), z).start())
    kv_all[z * 2 + xh] = kv_src[z]
    x_copy(z, xh).start()
    loop(1, 16, lambda i: h_copy(lax.rem(grp + i, 16), grp).start())

    loads[4].wait()
    scale = jnp.asarray(HD**-0.5, BF)
    for c in range(HEADS // 2):
        qq = q_in[:, c * TOK : (c + 1) * TOK] * scale
        top, bot = qq[:HALF], qq[HALF:]
        q_src[2 * c] = jnp.where(low_half, top, swap(bot))
        q_src[2 * c + 1] = jnp.where(low_half, swap(top), bot)
    loop(0, NZ - 1, lambda i: q_copy(far(i), z).start())
    q_all[z] = q_src[z]

    length = len_ref[0]

    def place(kv, rows, at, live):
        column = lane(rows)
        bias = jnp.where(live, 0.0, DEAD).astype(BF)
        k2[pl.ds(at, rows), :] = jnp.where(column < HD, kv, jnp.where(column == HD, bias, jnp.zeros_like(bias)))
        ones = jnp.where(column == HD, 1.0, 0.0).astype(BF)
        v2[pl.ds(at, rows), :] = jnp.where(column < HD, swap(kv), ones)

    def place_own(slot):
        at = pl.multiple_of(slot * TOK, TOK)
        pos = slot * TOK + lax.broadcasted_iota(jnp.int32, (TOK, TOK), 0)
        place(kv_all[slot], TOK, at, pos < length)

    place_own(z * 2 + xh)

    def on_kv(i):
        t = far(i)
        kv_copy(t, t).wait_recv()
        x_copy(t, xh).start()
        place_own(t * 2 + xh)

    loop(0, NZ - 1, on_kv)

    h_all[grp] = h_src[...]
    loop(1, 16, lambda i: h_copy(lax.rem(grp + i, 16), lax.rem(grp + i, 16)).wait_recv())
    for b in range(16):
        flag = jnp.full((HROWS, TOK), mask_ref[0, b // 2], jnp.int32) > 0
        place(h_all[b], HROWS, OWN + b * HROWS, flag)

    x_copy(z, 1 - xh).wait_recv()
    place_own(z * 2 + 1 - xh)

    def on_x(i):
        t = far(i)
        x_copy(t, 1 - xh).wait_recv()
        place_own(t * 2 + 1 - xh)

    loop(0, NZ - 1, on_x)

    def open_q(t):
        packed = q_all[t]
        one = jnp.where(lane(HALF) == HD, 1.0, 0.0).astype(BF)
        return [jnp.where(low_half, packed, one), jnp.where(low_half, swap(packed), one)]

    def close_o(rows):
        return jnp.where(low_half, rows[:HALF], swap(rows[HALF:]))

    rows = 2 * TOK
    chunk = 1024

    def attend(j):
        first = lax.rem(z + 8 + j, NZ)
        second = lax.rem(z + 8 - j + NZ, NZ)
        second = jnp.where(j == 0, z, second)
        q_copy(first, first).wait_recv()

        @pl.when(j != 0)
        def _():
            q_copy(second, second).wait_recv()

        q2 = jnp.concatenate(open_q(first) + open_q(second), axis=0)
        best = jnp.full((rows, TOK), -jnp.inf, jnp.float32)
        for c in range(0, KEYS, chunk):
            scores = lax.dot_general(
                q2, k2[c : c + chunk, :], (((1,), (1,)), ((), ())), preferred_element_type=jnp.float32
            )
            s_ref[:, c : c + chunk] = scores
            for n in range(0, chunk, TOK):
                best = jnp.maximum(best, scores[:, n : n + TOK])
        top = jnp.max(best, axis=1, keepdims=True)
        mixed = jnp.zeros((rows, TOK), jnp.float32)
        for c in range(0, KEYS, chunk):
            weights = jnp.exp(s_ref[:, c : c + chunk] - top).astype(BF)
            mixed += jnp.dot(weights, v2[c : c + chunk, :], preferred_element_type=jnp.float32)
        out = (mixed / mixed[:, HD : HD + 1]).astype(BF)
        o_src[first] = close_o(out[:TOK])
        o_copy(first, z).start()

        @pl.when(j == 0)
        def _():
            o_all[z] = close_o(out[TOK:])

        @pl.when(j != 0)
        def _():
            o_src[second] = close_o(out[TOK:])
            o_copy(second, z).start()

    loop(0, 8, attend)

    loop(0, NZ - 1, lambda i: o_copy(far(i), far(i)).wait_recv())
    for c in range(HEADS // 2):
        a, b = o_all[2 * c], o_all[2 * c + 1]
        cols = slice(c * TOK, (c + 1) * TOK)
        o_ref[0, :HALF, cols] = jnp.where(low_half, a, swap(b))
        o_ref[0, HALF:, cols] = jnp.where(low_half, swap(a), b)

    loop(0, NZ - 1, lambda i: kv_copy(far(i), z).wait_send())
    loop(0, NZ, lambda i: x_copy(i, xh).wait_send())
    loop(1, 16, lambda i: h_copy(lax.rem(grp + i, 16), grp).wait_send())
    loop(0, NZ - 1, lambda i: q_copy(far(i), z).wait_send())
    loop(0, NZ - 1, lambda i: o_copy(far(i), z).wait_send())


def body(queries, keys, values, hist_keys, hist_values, lengths, hist_mask):
    hbm = pl.BlockSpec(memory_space=pl.ANY)
    smem = pl.BlockSpec(memory_space=pltpu.SMEM)
    dma = pltpu.SemaphoreType.DMA
    vmem = pltpu.VMEM
    ch = HEADS * HD
    return pl.pallas_call(
        kernel,
        out_shape=jax.ShapeDtypeStruct((1, TOK, ch), BF),
        in_specs=[hbm] * 5 + [smem] * 2,
        out_specs=pl.BlockSpec(memory_space=pltpu.VMEM),
        scratch_shapes=[
            vmem((TOK, ch), BF), vmem((TOK, ch), BF), vmem((TOK, ch), BF),
            vmem((HROWS, TOK), BF), vmem((HROWS, TOK), BF),
            vmem((HEADS, TOK, TOK), BF), vmem((SLOTS, TOK, TOK), BF),
            vmem((HROWS, TOK), BF), vmem((16, HROWS, TOK), BF),
            vmem((NZ, HALF, TOK), BF), vmem((NZ, HALF, TOK), BF),
            vmem((NZ, HALF, TOK), BF), vmem((NZ, HALF, TOK), BF),
            vmem((KEYS, TOK), BF), vmem((KEYS, TOK), BF),
            vmem((2 * TOK, KEYS), jnp.float32),
            dma((5,)), *[dma((16,))] * 10,
        ],
        compiler_params=pltpu.CompilerParams(
            collective_id=0, has_side_effects=True, vmem_limit_bytes=48 * 2**20
        ),
        cost_estimate=pl.CostEstimate(
            flops=4 * 2048 * KEYS * HD, bytes_accessed=2**20, transcendentals=2048 * KEYS
        ),
    )(queries, keys, values, hist_keys, hist_values, lengths, hist_mask)


def solution(mesh):
    return jax.shard_map(
        body,
        mesh=mesh,
        in_specs=(
            P("grp", "seq", None),
            P("grp", "seq", None),
            P("grp", "seq", None),
            P("grp", None),
            P("grp", None),
            P("grp"),
            P("grp", None),
        ),
        out_specs=P("grp", "seq", None),
        check_vma=False,
    )
```

time: 214 us -> 76.3 us (0.36)
  blocking collectives: 75.2 us -> 0 us
  Pallas kernels: 0 us -> 69.8 us
  waiting for transfers between devices: 51.5 us -> 0 us
  starting transfers between devices: 28.5 us -> 0 us
  other arithmetic: 24.2 us -> 0 us
  matrix products: 16.2 us -> 0 us
  local copies, waits for them, and re-layouts: 16.5 us -> 5.36 us
    pallas_call x0 -> x1, Pallas kernels: none -> 69.8 us  [body(): pl.pallas_call(kernel, out_shape=jax.ShapeDtypeStruct((1, TOK, ch), BF),...]
    all_to_all x3 -> x0, waiting for transfers between devices: 51.5 us -> none  [the longest x1 31.1 us: body(): lax.all_to_all(twice_k, 'seq', split_axis=0, concat_axis=1, tiled=True)]
    all_gather x2 -> x0, blocking collectives: 39 us -> none  [the longest x1 21.1 us: body(): lax.all_gather(slice_v, 'grp', axis=0, tiled=True)]
    all_to_all x1 -> x0, blocking collectives: 36.2 us -> none  [body(): lax.all_to_all(head_out, 'seq', split_axis=1, concat_axis=0, tiled=True)]
    all_to_all x3 -> x0, starting transfers between devices: 28.5 us -> none  [the longest x1 18.2 us: body(): lax.all_to_all(local_q, 'seq', split_axis=0, concat_axis=1, tiled=True)]
    dot_general x8 -> x0, matrix products: 16.2 us -> none  [the longest x4 9.76 us: one_block(): mixed = jnp.dot(rounded, value_rows, preferred_element_type=jnp.float32)]
    unnamed x1 -> x0, other arithmetic: 11.8 us -> none
    reduce_sum x4 -> x0, other arithmetic: 11.6 us -> none  [one_block(): total = jnp.sum(weights, axis=1, keepdims=True)]
  transfers between devices with their start and end apart: 3 -> 0, of which waited for: 2 -> 0; matrix products, arithmetic and copies ran while one was open for 3% -> 0% of each run, Pallas kernels for 0% -> 0%
where the time goes in v1:
time: 76.3 us; the launch traced here: 75.8 us
  Pallas kernels  69.8 us (91%)
  local copies, waits for them, and re-layouts  5.36 us (7%)
    pallas_call x1, Pallas kernels, body(): pl.pallas_call(kernel, out_shape=jax.ShapeDtypeStruct((1, TOK, ch), BF),...  69.8 us
    unnamed x13, local copies, waits for them, and re-layouts  5.36 us

profile of v1, /device:TPU:6, one launch (start us, length us, event | category | flops | bytes accessed | tf_op | source)
XLA Modules:
  0.0 75.8 jit_solution(366939094936140647)
XLA Ops:
  0.0 0.0 copy-start.5
  0.7 0.0 copy-done.5
  0.7 0.0 copy-start
  0.7 0.9 %copy-done = bf16[1,128,1024]{2,1,0:T(8,128)(2,1)S(1)} copy-done((bf16[1,128,1024]{2,1,0:T(8,128)(2,1)S(1)}, bf16[1,128,1024]{2,1,0:T(8,128)(2,1)}, u32[]{:S(2)}) %copy-start) | copy-done | bytes 262168
  1.6 0.0 copy-start.1
  1.6 0.9 %copy-done.1 = bf16[1,128,1024]{2,1,0:T(8,128)(2,1)S(1)} copy-done((bf16[1,128,1024]{2,1,0:T(8,128)(2,1)S(1)}, bf16[1,128,1024]{2,1,0:T(8,128)(2,1)}, u32[]{:S(2)}) %copy-start.1) | copy-done | bytes 262168
  2.6 0.0 copy-start.2
  2.6 0.9 %copy-done.2 = bf16[1,128,1024]{2,1,0:T(8,128)(2,1)S(1)} copy-done((bf16[1,128,1024]{2,1,0:T(8,128)(2,1)S(1)}, bf16[1,128,1024]{2,1,0:T(8,128)(2,1)}, u32[]{:S(2)}) %copy-start.2) | copy-done | bytes 262168
  3.5 0.0 copy-start.3
  3.5 0.9 %copy-done.3 = bf16[64,1024]{1,0:T(8,128)(2,1)S(1)} copy-done((bf16[64,1024]{1,0:T(8,128)(2,1)S(1)}, bf16[64,1024]{1,0:T(8,128)(2,1)}, u32[]{:S(2)}) %copy-start.3) | copy-done | bytes 131096
  4.4 0.0 copy-start.4
  4.4 0.9 %copy-done.4 = bf16[64,1024]{1,0:T(8,128)(2,1)S(1)} copy-done((bf16[64,1024]{1,0:T(8,128)(2,1)S(1)}, bf16[64,1024]{1,0:T(8,128)(2,1)}, u32[]{:S(2)}) %copy-start.4) | copy-done | bytes 131096
  5.3 69.8 %shard_map.73 = bf16[1,128,1024]{2,1,0:T(8,128)(2,1)S(1)} custom-call(bf16[1,128,1024]{2,1,0:T(8,128)(2,1)S(1)} %copy-done, bf16[1,128,1024]{2,1,0:T(8,128)(2,1)S(1)} %copy-done.1, bf16[1,128,1024]{2,1,0:T(8,128)(2,1)S(1)} %copy-done.2, bf16[64,1024]{1,0:T(8,128)(2,1)S(1)} %copy-done.3, bf16[64,1024]{1,0:T(8,128)(2,1)S(1)} %copy-done.4, s32[1]{0:T(128)S(6)} %copy.9.len_ref, ...), custom_call_target="tpu_custom_call" | custom-call | flops 2684354560 | bytes 1048576 | tf_op jit(solution)/shard_map/pallas_call | solution.py:263
  75.1 0.7 copy.10
Async XLA Ops:
  0.0 0.7 copy-start.5
  0.7 1.0 %copy-start = (bf16[1,128,1024]{2,1,0:T(8,128)(2,1)S(1)}, bf16[1,128,1024]{2,1,0:T(8,128)(2,1)}, u32[]{:S(2)}) copy-start(bf16[1,128,1024]{2,1,0:T(8,128)(2,1)} %q_hbm.1) | copy-start | bytes 786436
  1.6 0.9 %copy-start.1 = (bf16[1,128,1024]{2,1,0:T(8,128)(2,1)S(1)}, bf16[1,128,1024]{2,1,0:T(8,128)(2,1)}, u32[]{:S(2)}) copy-start(bf16[1,128,1024]{2,1,0:T(8,128)(2,1)} %k_hbm.1) | copy-start | bytes 786436
  2.6 0.9 %copy-start.2 = (bf16[1,128,1024]{2,1,0:T(8,128)(2,1)S(1)}, bf16[1,128,1024]{2,1,0:T(8,128)(2,1)}, u32[]{:S(2)}) copy-start(bf16[1,128,1024]{2,1,0:T(8,128)(2,1)} %v_hbm.1) | copy-start | bytes 786436
  3.5 0.9 %copy-start.3 = (bf16[64,1024]{1,0:T(8,128)(2,1)S(1)}, bf16[64,1024]{1,0:T(8,128)(2,1)}, u32[]{:S(2)}) copy-start(bf16[64,1024]{1,0:T(8,128)(2,1)} %hk_hbm.1) | copy-start | bytes 393220
  4.4 0.9 %copy-start.4 = (bf16[64,1024]{1,0:T(8,128)(2,1)S(1)}, bf16[64,1024]{1,0:T(8,128)(2,1)}, u32[]{:S(2)}) copy-start(bf16[64,1024]{1,0:T(8,128)(2,1)} %hv_hbm.1) | copy-start | bytes 393220

commit v2 on v1

v2 whole, which is shorter than its diff:
```python
import jax
import jax.numpy as jnp
from jax import lax
from jax.experimental import pallas as pl
from jax.experimental.pallas import tpu as pltpu
from jax.sharding import PartitionSpec as P

HD = 64
HEADS = 16
NZ = 16
TOK = 128
HALF = TOK // 2
SLOTS = 32
HROWS = 64
HIST = 1024
OWN = NZ * TOK
FIRST = OWN + HIST
KEYS = OWN + FIRST
AHEAD = 4
DEAD = -1e30
WINDOW = 8
MESH = pl.DeviceIdType.MESH
BF = jnp.bfloat16


def swap(x):
    return pltpu.roll(x, HD, 1)


def kernel(
    q_hbm, k_hbm, v_hbm, hk_hbm, hv_hbm, len_hbm, mask_hbm, o_ref,
    q_in, k_in, v_in, hk_in, hv_in,
    kv_src, kv_all, h_all, q_src, q_all, o_src, o_all,
    k2, v2, s_ref, acc_ref, top_ref, len_ref, mask_ref,
    in_sem, kv_rs, x_rs, h_rs, q_rs, kv_ss, x_ss, h_ss, q_ss, o_ss, o_rs,
):
    grp = lax.axis_index("grp")
    seq = lax.axis_index("seq")
    z = seq // 2
    xh = lax.rem(seq, 2)
    hcol = pl.multiple_of(z // 2 * TOK, TOK)
    odd = lax.rem(z, 2)

    loads = [
        pltpu.make_async_copy(k_hbm.at[0], k_in, in_sem.at[0]),
        pltpu.make_async_copy(v_hbm.at[0], v_in, in_sem.at[1]),
        pltpu.make_async_copy(hk_hbm.at[:, pl.ds(hcol, TOK)], hk_in, in_sem.at[2]),
        pltpu.make_async_copy(hv_hbm.at[:, pl.ds(hcol, TOK)], hv_in, in_sem.at[3]),
        pltpu.make_async_copy(q_hbm.at[0], q_in, in_sem.at[4]),
        pltpu.make_async_copy(len_hbm, len_ref, in_sem.at[5]),
        pltpu.make_async_copy(mask_hbm, mask_ref, in_sem.at[6]),
    ]
    for load in loads:
        load.start()

    def z_peer(t):
        return {"seq": t * 2 + xh}

    barrier = pltpu.get_barrier_semaphore()

    def far(i):
        return lax.rem(z + 8 + (1 - 2 * lax.rem(i, 2)) * ((i + 1) // 2), NZ)

    def greet_z(i, c):
        pl.semaphore_signal(barrier, inc=1, device_id=z_peer(far(i)), device_id_type=MESH)
        return c

    lax.fori_loop(0, NZ - 1, greet_z, 0)
    pl.semaphore_signal(barrier, inc=1, device_id={"seq": z * 2 + 1 - xh}, device_id_type=MESH)

    y = grp // 4
    pair = grp + 1 - 2 * lax.rem(grp, 2)
    side = grp + 2 - 4 * lax.rem(grp // 2, 2)

    def y_peer(i):
        return lax.rem(grp + 4 * i, 16)

    for peer in (pair, side, y_peer(1), y_peer(2), y_peer(3)):
        pl.semaphore_signal(barrier, inc=1, device_id={"grp": peer}, device_id_type=MESH)

    def lane(rows):
        return lax.broadcasted_iota(jnp.int32, (rows, TOK), 1)

    low = lane(TOK) < HD
    low_half = lane(HALF) < HD

    loads[0].wait()
    loads[1].wait()
    for c in range(HEADS // 2):
        kk = k_in[:, c * TOK : (c + 1) * TOK]
        vv = v_in[:, c * TOK : (c + 1) * TOK]
        kv_src[2 * c] = jnp.where(low, kk, swap(vv))
        kv_src[2 * c + 1] = jnp.where(low, swap(kk), vv)
    loads[2].wait()
    loads[3].wait()
    hk = hk_in[...]
    hv = hv_in[...]
    even_h = jnp.where(low_half, hk, swap(hv))
    odd_h = jnp.where(low_half, swap(hk), hv)
    pick = jnp.full((HROWS, TOK), odd, jnp.int32) == 1
    h_all[grp] = jnp.where(pick, odd_h, even_h)

    pl.semaphore_wait(barrier, 21)

    def kv_copy(t, slot):
        return pltpu.make_async_remote_copy(
            src_ref=kv_src.at[t], dst_ref=kv_all.at[slot * 2 + xh],
            send_sem=kv_ss, recv_sem=kv_rs.at[slot],
            device_id=z_peer(t), device_id_type=MESH,
        )

    def x_copy(t, side):
        return pltpu.make_async_remote_copy(
            src_ref=kv_all.at[t * 2 + side], dst_ref=kv_all.at[t * 2 + side],
            send_sem=x_ss, recv_sem=x_rs.at[t],
            device_id={"seq": z * 2 + 1 - xh}, device_id_type=MESH,
        )

    def h_copy(peer, base, count, recv):
        part = h_all.at[pl.ds(base, count)]
        return pltpu.make_async_remote_copy(
            src_ref=part, dst_ref=part, send_sem=h_ss, recv_sem=h_rs.at[recv],
            device_id={"grp": peer}, device_id_type=MESH,
        )

    two = grp // 2 * 2
    h_sends = [h_copy(pair, grp, 1, 0), h_copy(side, two, 2, 1)]
    h_sends += [h_copy(y_peer(i), y * 4, 4, 1 + i) for i in (1, 2, 3)]
    h_recvs = [h_copy(pair, pair, 1, 0), h_copy(side, side // 2 * 2, 2, 1)]
    h_recvs += [h_copy(y_peer(i), y_peer(4 - i) // 4 * 4, 4, 1 + i) for i in (1, 2, 3)]

    def q_copy(t, slot):
        return pltpu.make_async_remote_copy(
            src_ref=q_src.at[t], dst_ref=q_all.at[slot],
            send_sem=q_ss, recv_sem=q_rs.at[slot],
            device_id=z_peer(t), device_id_type=MESH,
        )

    def o_copy(t, slot):
        return pltpu.make_async_remote_copy(
            src_ref=o_src.at[t], dst_ref=o_all.at[slot],
            send_sem=o_ss, recv_sem=o_rs,
            device_id=z_peer(t), device_id_type=MESH,
        )

    def loop(lo, hi, f):
        def step(i, c):
            f(i)
            return c

        lax.fori_loop(lo, hi, step, 0)

    loop(0, WINDOW, lambda i: kv_copy(far(i), z).start())
    kv_all[z * 2 + xh] = kv_src[z]
    x_copy(z, xh).start()
    h_sends[0].start()

    loads[4].wait()
    scale = jnp.asarray(HD**-0.5, BF)
    for c in range(HEADS // 2):
        qq = q_in[:, c * TOK : (c + 1) * TOK] * scale
        top, bot = qq[:HALF], qq[HALF:]
        q_src[2 * c] = jnp.where(low_half, top, swap(bot))
        q_src[2 * c + 1] = jnp.where(low_half, swap(top), bot)
    q_all[z] = q_src[z]
    q_copy(lax.rem(z + 12, NZ), z).start()
    loop(9, 15, lambda i: q_copy(far(i), z).start())
    h_recvs[0].wait_recv()
    h_sends[1].start()

    loads[5].wait()
    loads[6].wait()
    length = len_ref[0]

    def prepare(rows, at, live):
        column = lane(rows)
        k2[pl.ds(at, rows), :] = jnp.where((column == HD) & jnp.logical_not(live), DEAD, 0.0).astype(BF)
        v2[pl.ds(at, rows), :] = jnp.where(column == HD, 1.0, 0.0).astype(BF)

    def prepare_own(t, side_x, base):
        pos = (t * 2 + side_x) * TOK + lax.broadcasted_iota(jnp.int32, (TOK, TOK), 0)
        prepare(TOK, pl.multiple_of(base + t * TOK, TOK), pos < length)

    def prepare_both(t):
        prepare_own(t, xh, 0)
        prepare_own(t, 1 - xh, FIRST)

    loop(0, NZ, prepare_both)
    for b in range(HIST // TOK):
        prepare(TOK, OWN + b * TOK, jnp.full((TOK, TOK), mask_ref[0, b], jnp.int32) > 0)

    def place(kv, rows, at):
        k2[pl.ds(at, rows), :HD] = kv[:, :HD]
        v2[pl.ds(at, rows), :HD] = kv[:, HD:]

    def place_own(t, side_x, base):
        place(kv_all[t * 2 + side_x], TOK, pl.multiple_of(base + t * TOK, TOK))

    place_own(z, xh, 0)
    h_recvs[1].wait_recv()
    for send in h_sends[2:]:
        send.start()

    def on_kv(i):
        t = far(i)
        kv_copy(t, t).wait_recv()
        x_copy(t, xh).start()

        @pl.when(i < NZ - 1 - WINDOW)
        def _():
            kv_copy(far(i + WINDOW), z).start()

        @pl.when(i >= 7)
        def _():
            q_copy(far(i - 7), z).start()

        place_own(t, xh, 0)

    loop(0, NZ - 1, on_kv)

    for recv in h_recvs[2:]:
        recv.wait_recv()
    for b in range(16):
        place(h_all[b], HROWS, OWN + b * HROWS)

    def open_q(t):
        packed = q_all[t]
        one = jnp.where(lane(HALF) == HD, 1.0, 0.0).astype(BF)
        return [jnp.where(low_half, packed, one), jnp.where(low_half, swap(packed), one)]

    def close_o(rows):
        return jnp.where(low_half, rows[:HALF], swap(rows[HALF:]))

    rows = 2 * TOK
    chunk = 1024

    def sources(j):
        away = jnp.where(j < 3, j + 1, jnp.where(j == 3, 4, jnp.where(j == 4, 7, jnp.where(j == 5, 8, 11 - j + 1))))
        first = lax.rem(z + away, NZ)
        second = jnp.where(j == 3, z, jnp.where(j == 5, lax.rem(z + 12, NZ), lax.rem(z + NZ - away, NZ)))
        return first, second

    def query_rows(j):
        first, second = sources(j)
        return jnp.concatenate(open_q(first) + open_q(second), axis=0)

    def wait_q(j):
        first, second = sources(j)
        q_copy(first, first).wait_recv()

        @pl.when(j != 3)
        def _():
            q_copy(second, second).wait_recv()

    def part(q2, lo, hi):
        best = jnp.full((rows, TOK), -jnp.inf, jnp.float32)
        for c in range(lo, hi, chunk):
            scores = lax.dot_general(
                q2, k2[c : c + chunk, :], (((1,), (1,)), ((), ())), preferred_element_type=jnp.float32
            )
            s_ref[:, c : c + chunk] = scores
            for n in range(0, chunk, TOK):
                best = jnp.maximum(best, scores[:, n : n + TOK])
        top = jnp.max(best, axis=1, keepdims=True)
        mixed = jnp.zeros((rows, TOK), jnp.float32)
        for c in range(lo, hi, chunk):
            weights = jnp.exp(s_ref[:, c : c + chunk] - top).astype(BF)
            mixed += jnp.dot(weights, v2[c : c + chunk, :], preferred_element_type=jnp.float32)
        return mixed, top

    def finish(j, mixed):
        first, second = sources(j)
        out = (mixed / mixed[:, HD : HD + 1]).astype(BF)
        o_src[first] = close_o(out[:TOK])
        o_copy(first, z).start()

        @pl.when(j == 3)
        def _():
            o_all[z] = close_o(out[TOK:])

        @pl.when(j != 3)
        def _():
            o_src[second] = close_o(out[TOK:])
            o_copy(second, z).start()

    def begin(j):
        wait_q(j)
        mixed, top = part(query_rows(j), 0, FIRST)
        acc_ref[j] = mixed
        top_ref[j] = jnp.broadcast_to(top, (rows, TOK))

    loop(0, AHEAD, begin)

    x_copy(z, 1 - xh).wait_recv()
    place_own(z, 1 - xh, FIRST)

    def on_x(i):
        t = far(i)
        x_copy(t, 1 - xh).wait_recv()
        place_own(t, 1 - xh, FIRST)

    loop(0, NZ - 1, on_x)

    def merge(j):
        mixed, top = part(query_rows(j), FIRST, KEYS)
        before = top_ref[j]
        both = jnp.maximum(before, top)
        finish(j, acc_ref[j] * jnp.exp(before - both) + mixed * jnp.exp(top - both))

    def whole(j):
        wait_q(j)
        mixed, top = part(query_rows(j), 0, KEYS)
        finish(j, mixed)

    loop(AHEAD, 8, whole)
    loop(0, AHEAD, lambda i: merge(jnp.where(i < 2, 2 + i, 3 - i)))

    arrived = o_all.at[pl.ds(0, NZ - 1)]
    pltpu.make_async_remote_copy(
        src_ref=arrived, dst_ref=arrived, send_sem=o_ss, recv_sem=o_rs,
        device_id=z_peer(far(0)), device_id_type=MESH,
    ).wait_recv()
    for c in range(HEADS // 2):
        a, b = o_all[2 * c], o_all[2 * c + 1]
        cols = slice(c * TOK, (c + 1) * TOK)
        o_ref[0, :HALF, cols] = jnp.where(low_half, a, swap(b))
        o_ref[0, HALF:, cols] = jnp.where(low_half, swap(a), b)

    def drain(ref, count, sem):
        part = ref.at[pl.ds(0, count)]
        pltpu.make_async_remote_copy(
            src_ref=part, dst_ref=part, send_sem=sem, recv_sem=o_rs,
            device_id=z_peer(far(0)), device_id_type=MESH,
        ).wait_send()

    drain(kv_src, NZ - 1, kv_ss)
    drain(kv_all, NZ, x_ss)
    drain(h_all, 15, h_ss)
    drain(q_src, NZ - 1, q_ss)
    drain(o_src, NZ - 1, o_ss)


def body(queries, keys, values, hist_keys, hist_values, lengths, hist_mask):
    hbm = pl.BlockSpec(memory_space=pl.ANY)
    smem = pltpu.SMEM
    dma = pltpu.SemaphoreType.DMA
    vmem = pltpu.VMEM
    ch = HEADS * HD
    return pl.pallas_call(
        kernel,
        out_shape=jax.ShapeDtypeStruct((1, TOK, ch), BF),
        in_specs=[hbm] * 7,
        out_specs=pl.BlockSpec(memory_space=pltpu.VMEM),
        scratch_shapes=[
            vmem((TOK, ch), BF), vmem((TOK, ch), BF), vmem((TOK, ch), BF),
            vmem((HROWS, TOK), BF), vmem((HROWS, TOK), BF),
            vmem((HEADS, TOK, TOK), BF), vmem((SLOTS, TOK, TOK), BF),
            vmem((16, HROWS, TOK), BF),
            vmem((NZ, HALF, TOK), BF), vmem((NZ, HALF, TOK), BF),
            vmem((NZ, HALF, TOK), BF), vmem((NZ, HALF, TOK), BF),
            vmem((KEYS, TOK), BF), vmem((KEYS, TOK), BF),
            vmem((2 * TOK, KEYS), jnp.float32),
            vmem((AHEAD, 2 * TOK, TOK), jnp.float32), vmem((AHEAD, 2 * TOK, TOK), jnp.float32),
            smem((1,), jnp.int32), smem((1, 8), jnp.int32),
            dma((7,)), dma((16,)), dma((16,)), dma((5,)), dma((16,)), *[dma(())] * 6,
        ],
        compiler_params=pltpu.CompilerParams(
            collective_id=0, has_side_effects=True, vmem_limit_bytes=63 * 2**20
        ),
        cost_estimate=pl.CostEstimate(
            flops=4 * 2048 * KEYS * HD, bytes_accessed=2**20, transcendentals=2048 * KEYS
        ),
    )(queries, keys, values, hist_keys, hist_values, lengths, hist_mask)


def solution(mesh):
    return jax.shard_map(
        body,
        mesh=mesh,
        in_specs=(
            P("grp", "seq", None),
            P("grp", "seq", None),
            P("grp", "seq", None),
            P("grp", None),
            P("grp", None),
            P("grp"),
            P("grp", None),
        ),
        out_specs=P("grp", "seq", None),
        check_vma=False,
    )
```

time: 76.3 us -> 70.7 us (0.927)
  local copies, waits for them, and re-layouts: 5.36 us -> 1.67 us
  Pallas kernels: 69.8 us -> 68 us
    unnamed x13 -> x1, local copies, waits for them, and re-layouts: 5.36 us -> 1.67 us
    pallas_call x1, Pallas kernels: 69.8 us -> 68 us  [body(): pl.pallas_call(kernel, out_shape=jax.ShapeDtypeStruct((1, TOK, ch), BF),...]
where the time goes in v2:
time: 70.7 us; the launch traced here: 70.4 us
  Pallas kernels  68 us (96%)
  local copies, waits for them, and re-layouts  1.67 us (2%)
    pallas_call x1, Pallas kernels, body(): pl.pallas_call(kernel, out_shape=jax.ShapeDtypeStruct((1, TOK, ch), BF),...  68 us
    unnamed x1, local copies, waits for them, and re-layouts  1.67 us

profile of v2, /device:TPU:6, one launch (start us, length us, event | category | flops | bytes accessed | tf_op | source)
XLA Modules:
  0.0 70.4 jit_solution(6421077190931896689)
XLA Ops:
  0.7 68.0 %shard_map.73 = bf16[1,128,1024]{2,1,0:T(8,128)(2,1)} custom-call(bf16[1,128,1024]{2,1,0:T(8,128)(2,1)} %q_hbm.1, bf16[1,128,1024]{2,1,0:T(8,128)(2,1)} %k_hbm.1, bf16[1,128,1024]{2,1,0:T(8,128)(2,1)} %v_hbm.1, bf16[64,1024]{1,0:T(8,128)(2,1)} %hk_hbm.1, bf16[64,1024]{1,0:T(8,128)(2,1)} %hv_hbm.1, s32[1]{0:T(128)S(6)} %copy.9.len_hbm, s32[1,8]{1,0:T(1,128)} %mask_hbm.1), custom_call_target="tpu_custom_call" | custom-call | flops 2684354560 | bytes 1048576 | tf_op jit(solution)/shard_map/pallas_call | solution.py:349
  68.7 1.7 %copy.10 = bf16[1,128,1024]{2,1,0:T(8,128)(2,1)} copy(bf16[1,128,1024]{2,1,0:T(8,128)(2,1)} %shard_map.73) | data formatting | bytes 524288

commit v3 on v2

--- a/solution.py
+++ b/solution.py
@@ -28,9 +28,9 @@
 
 
 def kernel(
-    q_hbm, k_hbm, v_hbm, hk_hbm, hv_hbm, len_hbm, mask_hbm, o_ref,
+    q_hbm, k_hbm, v_hbm, hk_hbm, hv_hbm, len_hbm, mask_hbm, o_all,
     q_in, k_in, v_in, hk_in, hv_in,
-    kv_src, kv_all, h_all, q_src, q_all, o_src, o_all,
+    kv_src, kv_all, h_all, q_src, q_all, o_src,
     k2, v2, s_ref, acc_ref, top_ref, len_ref, mask_ref,
     in_sem, kv_rs, x_rs, h_rs, q_rs, kv_ss, x_ss, h_ss, q_ss, o_ss, o_rs,
 ):
@@ -268,6 +268,8 @@
             mixed += jnp.dot(weights, v2[c : c + chunk, :], preferred_element_type=jnp.float32)
         return mixed, top
 
+    own_out = pltpu.make_async_copy(o_src.at[z], o_all.at[z], in_sem.at[7])
+
     def finish(j, mixed):
         first, second = sources(j)
         out = (mixed / mixed[:, HD : HD + 1]).astype(BF)
@@ -276,7 +278,8 @@
 
         @pl.when(j == 3)
         def _():
-            o_all[z] = close_o(out[TOK:])
+            o_src[z] = close_o(out[TOK:])
+            own_out.start()
 
         @pl.when(j != 3)
         def _():
@@ -312,19 +315,23 @@
         mixed, top = part(query_rows(j), 0, KEYS)
         finish(j, mixed)
 
-    loop(AHEAD, 8, whole)
-    loop(0, AHEAD, lambda i: merge(jnp.where(i < 2, 2 + i, 3 - i)))
+    def answer(i):
+        @pl.when((i < 1) | (i > 4))
+        def _():
+            merge(jnp.where(i < 1, 2, jnp.where(i == 5, 3, 7 - i)))
+
+        @pl.when((i >= 1) & (i <= 4))
+        def _():
+            whole(i + 3)
+
+    loop(0, 8, answer)
 
     arrived = o_all.at[pl.ds(0, NZ - 1)]
     pltpu.make_async_remote_copy(
         src_ref=arrived, dst_ref=arrived, send_sem=o_ss, recv_sem=o_rs,
         device_id=z_peer(far(0)), device_id_type=MESH,
     ).wait_recv()
-    for c in range(HEADS // 2):
-        a, b = o_all[2 * c], o_all[2 * c + 1]
-        cols = slice(c * TOK, (c + 1) * TOK)
-        o_ref[0, :HALF, cols] = jnp.where(low_half, a, swap(b))
-        o_ref[0, HALF:, cols] = jnp.where(low_half, swap(a), b)
+    own_out.wait()
 
     def drain(ref, count, sem):
         part = ref.at[pl.ds(0, count)]
@@ -340,29 +347,37 @@
     drain(o_src, NZ - 1, o_ss)
 
 
+def unpack(slot_ref, o_ref):
+    low = lax.broadcasted_iota(jnp.int32, (HALF, TOK), 1) < HD
+    for c in range(slot_ref.shape[0] // 2):
+        a, b = slot_ref[2 * c], slot_ref[2 * c + 1]
+        cols = slice(c * TOK, (c + 1) * TOK)
+        o_ref[0, :HALF, cols] = jnp.where(low, a, swap(b))
+        o_ref[0, HALF:, cols] = jnp.where(low, swap(a), b)
+
+
 def body(queries, keys, values, hist_keys, hist_values, lengths, hist_mask):
     hbm = pl.BlockSpec(memory_space=pl.ANY)
     smem = pltpu.SMEM
     dma = pltpu.SemaphoreType.DMA
     vmem = pltpu.VMEM
     ch = HEADS * HD
-    return pl.pallas_call(
+    slots = pl.pallas_call(
         kernel,
-        out_shape=jax.ShapeDtypeStruct((1, TOK, ch), BF),
+        out_shape=jax.ShapeDtypeStruct((NZ, HALF, TOK), BF),
         in_specs=[hbm] * 7,
-        out_specs=pl.BlockSpec(memory_space=pltpu.VMEM),
+        out_specs=hbm,
         scratch_shapes=[
             vmem((TOK, ch), BF), vmem((TOK, ch), BF), vmem((TOK, ch), BF),
             vmem((HROWS, TOK), BF), vmem((HROWS, TOK), BF),
             vmem((HEADS, TOK, TOK), BF), vmem((SLOTS, TOK, TOK), BF),
             vmem((16, HROWS, TOK), BF),
-            vmem((NZ, HALF, TOK), BF), vmem((NZ, HALF, TOK), BF),
-            vmem((NZ, HALF, TOK), BF), vmem((NZ, HALF, TOK), BF),
+            vmem((NZ, HALF, TOK), BF), vmem((NZ, HALF, TOK), BF), vmem((NZ, HALF, TOK), BF),
             vmem((KEYS, TOK), BF), vmem((KEYS, TOK), BF),
             vmem((2 * TOK, KEYS), jnp.float32),
             vmem((AHEAD, 2 * TOK, TOK), jnp.float32), vmem((AHEAD, 2 * TOK, TOK), jnp.float32),
             smem((1,), jnp.int32), smem((1, 8), jnp.int32),
-            dma((7,)), dma((16,)), dma((16,)), dma((5,)), dma((16,)), *[dma(())] * 6,
+            dma((8,)), dma((16,)), dma((16,)), dma((5,)), dma((16,)), *[dma(())] * 6,
         ],
         compiler_params=pltpu.CompilerParams(
             collective_id=0, has_side_effects=True, vmem_limit_bytes=63 * 2**20
@@ -371,6 +386,15 @@
             flops=4 * 2048 * KEYS * HD, bytes_accessed=2**20, transcendentals=2048 * KEYS
         ),
     )(queries, keys, values, hist_keys, hist_values, lengths, hist_mask)
+    parts = 2
+    return pl.pallas_call(
+        unpack,
+        grid=(parts,),
+        out_shape=jax.ShapeDtypeStruct((1, TOK, ch), BF),
+        in_specs=[pl.BlockSpec((NZ // parts, HALF, TOK), lambda i: (i, 0, 0))],
+        out_specs=pl.BlockSpec((1, TOK, ch // parts), lambda i: (0, 0, i)),
+        compiler_params=pltpu.CompilerParams(vmem_limit_bytes=63 * 2**20),
+    )(slots)
 
 
 def solution(mesh):

time: 70.7 us -> 70 us (0.990)
  local copies, waits for them, and re-layouts: 1.67 us -> 0 us
  Pallas kernels: 68 us -> 69.1 us
    unnamed x1 -> x0, local copies, waits for them, and re-layouts: 1.67 us -> none
    pallas_call x1 -> x2, Pallas kernels: 68 us -> 69.1 us  [the longest x1 67.3 us: body(): pl.pallas_call(kernel, out_shape=jax.ShapeDtypeStruct((NZ, HALF, TOK), BF...]
where the time goes in v3:
time: 70 us; the launch traced here: 69.7 us
  Pallas kernels  69.1 us (99%)
    pallas_call x1, Pallas kernels, body(): pl.pallas_call(kernel, out_shape=jax.ShapeDtypeStruct((NZ, HALF, TOK), BF...  67.3 us
    pallas_call x1, Pallas kernels, body(): pl.pallas_call(unpack, grid=(parts,), out_shape=jax.ShapeDtypeStruct((1,...  1.79 us

profile of v3, /device:TPU:6, one launch (start us, length us, event | category | flops | bytes accessed | tf_op | source)
XLA Modules:
  0.0 69.7 jit_solution(11332251180165119401)
XLA Ops:
  0.7 67.3 %shard_map.73.slot_ref = bf16[16,64,128]{2,1,0:T(8,128)(2,1)} custom-call(bf16[1,128,1024]{2,1,0:T(8,128)(2,1)} %q_hbm.1, bf16[1,128,1024]{2,1,0:T(8,128)(2,1)} %k_hbm.1, bf16[1,128,1024]{2,1,0:T(8,128)(2,1)} %v_hbm.1, bf16[64,1024]{1,0:T(8,128)(2,1)} %hk_hbm.1, bf16[64,1024]{1,0:T(8,128)(2,1)} %hv_hbm.1, s32[1]{0:T(128)S(6)} %copy.8.len_hbm, s32[1,8]{1,0:T(1,128)} %mask_hbm.1), custom_call_target="tpu_custom_call" | custom-call | flops 2684354560 | bytes 1048576 | tf_op jit(solution)/shard_map/pallas_call | solution.py:365
  67.9 1.8 %shard_map.74 = bf16[1,128,1024]{2,1,0:T(8,128)(2,1)} custom-call(bf16[16,64,128]{2,1,0:T(8,128)(2,1)} %shard_map.73.slot_ref), custom_call_target="tpu_custom_call" | custom-call | tf_op jit(solution)/shard_map/pallas_call | solution.py:390

commit v4 on v3

--- a/solution.py
+++ b/solution.py
@@ -181,13 +181,7 @@
         pos = (t * 2 + side_x) * TOK + lax.broadcasted_iota(jnp.int32, (TOK, TOK), 0)
         prepare(TOK, pl.multiple_of(base + t * TOK, TOK), pos < length)
 
-    def prepare_both(t):
-        prepare_own(t, xh, 0)
-        prepare_own(t, 1 - xh, FIRST)
-
-    loop(0, NZ, prepare_both)
-    for b in range(HIST // TOK):
-        prepare(TOK, OWN + b * TOK, jnp.full((TOK, TOK), mask_ref[0, b], jnp.int32) > 0)
+    loop(0, NZ, lambda t: prepare_own(t, xh, 0))
 
     def place(kv, rows, at):
         k2[pl.ds(at, rows), :HD] = kv[:, :HD]
@@ -215,13 +209,17 @@
             q_copy(far(i - 7), z).start()
 
         place_own(t, xh, 0)
-
-    loop(0, NZ - 1, on_kv)
-
+        prepare_own(t, 1 - xh, FIRST)
+
+    prepare_own(z, 1 - xh, FIRST)
+    loop(0, 7, on_kv)
     for recv in h_recvs[2:]:
         recv.wait_recv()
+    for b in range(HIST // TOK):
+        prepare(TOK, OWN + b * TOK, jnp.full((TOK, TOK), mask_ref[0, b], jnp.int32) > 0)
     for b in range(16):
         place(h_all[b], HROWS, OWN + b * HROWS)
+    loop(7, NZ - 1, on_kv)
 
     def open_q(t):
         packed = q_all[t]

time: 70 us -> 69.9 us (level)
  no operation moved by 1% of the time
where the time goes in v4:
time: 69.9 us; the launch traced here: 69.5 us
  Pallas kernels  68.8 us (98%)
    pallas_call x1, Pallas kernels, body(): pl.pallas_call(kernel, out_shape=jax.ShapeDtypeStruct((NZ, HALF, TOK), BF...  67 us
    pallas_call x1, Pallas kernels, body(): pl.pallas_call(unpack, grid=(parts,), out_shape=jax.ShapeDtypeStruct((1,...  1.79 us

profile of v4, /device:TPU:6, one launch (start us, length us, event | category | flops | bytes accessed | tf_op | source)
XLA Modules:
  0.0 69.5 jit_solution(12369453838244021038)
XLA Ops:
  0.7 67.0 %shard_map.73.slot_ref = bf16[16,64,128]{2,1,0:T(8,128)(2,1)} custom-call(bf16[1,128,1024]{2,1,0:T(8,128)(2,1)} %q_hbm.1, bf16[1,128,1024]{2,1,0:T(8,128)(2,1)} %k_hbm.1, bf16[1,128,1024]{2,1,0:T(8,128)(2,1)} %v_hbm.1, bf16[64,1024]{1,0:T(8,128)(2,1)} %hk_hbm.1, bf16[64,1024]{1,0:T(8,128)(2,1)} %hv_hbm.1, s32[1]{0:T(128)S(6)} %copy.8.len_hbm, s32[1,8]{1,0:T(1,128)} %mask_hbm.1), custom_call_target="tpu_custom_call" | custom-call | flops 2684354560 | bytes 1048576 | tf_op jit(solution)/shard_map/pallas_call | solution.py:363
  67.7 1.8 %shard_map.74 = bf16[1,128,1024]{2,1,0:T(8,128)(2,1)} custom-call(bf16[16,64,128]{2,1,0:T(8,128)(2,1)} %shard_map.73.slot_ref), custom_call_target="tpu_custom_call" | custom-call | tf_op jit(solution)/shard_map/pallas_call | solution.py:388
